TPU v7x, 32 devices: a whole 2x2x4 slice. The times are simulated.
32 devices in a mesh: groups: 2 (over x), lat: 8 (over z, y), layer: 2 (over core).
Axes of the slice: x: 2, y: 2, z: 4, core: 2. Of those that a mesh axis runs over, the one named last changes fastest.
Arguments:
- streams: bfloat16 [2, 1024, 4096], P('layer', ('groups', 'lat')), parts along dimension 1, may hold values from -6 to 6
- enc_weight: bfloat16 [4, 4096, 8192], P(('groups', 'layer'), None, 'lat'), parts along dimension 0, may hold values from -0.0625 to 0.0625
- enc_bias: float32 [16384], P(('groups', 'lat')), parts along dimension 0, may hold values from -3 to 3
- dec_weight: bfloat16 [4, 8192, 4096], P(('groups', 'layer'), 'lat'), parts along dimension 0, may hold values from -0.198873782 to 0.198873782
- dec_bias: float32 [4, 4096], P(('groups', 'layer'), 'lat'), parts along dimension 0, may hold values from -3 to 3
Outputs:
- enc_grad: bfloat16 [4, 4096, 8192], P(('groups', 'layer'), None, 'lat'), parts along dimension 0
- enc_bias_grad: float32 [16384], P(('groups', 'lat')), parts along dimension 0
- dec_grad: bfloat16 [4, 8192, 4096], P(('groups', 'layer'), 'lat'), parts along dimension 0
- dec_bias_grad: float32 [4, 4096], P(('groups', 'layer'), 'lat'), parts along dimension 0
There are 2 independent parts, one for each index of `groups`. A program takes and returns all parts, laid end to end along the dimension named above; each array names one. Nothing has to cross between parts.
All inputs are finite; a program needn't handle non-finite values.
Results may differ from a plain program's by a relative error of at most 0.0055.
Values may be sent and summed in bfloat16 or wider, within the bound.
A program may use at most 128 MiB of HBM per device.

v0:
```python
import jax
import jax.numpy as jnp
from jax import lax
from jax.sharding import PartitionSpec as P

penalty_weight = 1.0
epsilon_sq = 1e-06


def per_device(streams, enc_weight, enc_bias, dec_weight, dec_bias):
    gathered = lax.all_gather(streams, "lat", axis=1, tiled=True)
    inputs_full = gathered[0]
    total_rows = inputs_full.shape[0]
    decoder = dec_weight[0]
    pre_part = jnp.dot(inputs_full, enc_weight[0], preferred_element_type=jnp.float32)
    row_norm = jnp.sqrt(jnp.sum(jnp.square(decoder.astype(jnp.float32)), axis=1) + epsilon_sq)
    pre_sum, strength = lax.psum((pre_part, row_norm), "layer")
    pre = pre_sum + enc_bias
    features = jax.nn.softplus(pre).astype(jnp.bfloat16)
    col_count = decoder.shape[1] // lax.axis_size("lat")
    offset = lax.axis_index("lat") * col_count
    own_cols = lax.dynamic_slice_in_dim(inputs_full, offset, col_count, 1)
    recon = lax.psum_scatter(
        lax.dot_general(
            decoder, features, (((0,), (1,)), ((), ())), preferred_element_type=jnp.float32
        ),
        "lat",
        scatter_dimension=0,
        tiled=True,
    )
    row_scale = 1.0 / jnp.sqrt(jnp.float32(total_rows))
    recon_err = recon + dec_bias[0][:, None] - own_cols.T.astype(jnp.float32)
    err_grad = recon_err * row_scale
    dec_bias_grad = jnp.sum(err_grad, axis=1)[None, :]
    err_round = err_grad.astype(jnp.bfloat16)
    err_full = lax.all_gather(err_round, "lat", axis=0, tiled=True)
    feat_part = lax.dot_general(
        err_full, decoder, (((0,), (1,)), ((), ())), preferred_element_type=jnp.float32
    )
    feat_sum = lax.psum(feat_part, "layer")
    direct = lax.dot_general(
        features, err_full, (((0,), (1,)), ((), ())), preferred_element_type=jnp.float32
    )
    feat_sums = jnp.sum(features.astype(jnp.float32), axis=0)
    shrink = (penalty_weight * row_scale * feat_sums / row_norm)[:, None] * decoder.astype(
        jnp.float32
    )
    dec_grad = (direct + shrink).astype(jnp.bfloat16)[None]
    feat_grad = feat_sum + penalty_weight * row_scale * strength
    pre_grad = feat_grad * jax.nn.sigmoid(pre)
    enc_bias_grad = jnp.sum(pre_grad, axis=0)
    pre_round = pre_grad.astype(jnp.bfloat16)
    enc_grad = lax.dot_general(
        inputs_full, pre_round, (((0,), (0,)), ((), ())), preferred_element_type=jnp.float32
    )
    return (enc_grad.astype(jnp.bfloat16)[None], enc_bias_grad, dec_grad, dec_bias_grad)


def solution(mesh):
    in_specs = (
        P("layer", ("groups", "lat"), None),
        P(("groups", "layer"), None, "lat"),
        P(("groups", "lat")),
        P(("groups", "layer"), "lat", None),
        P(("groups", "layer"), "lat"),
    )
    out_specs = (
        P(("groups", "layer"), None, "lat"),
        P(("groups", "lat")),
        P(("groups", "layer"), "lat", None),
        P(("groups", "layer"), "lat"),
    )
    return jax.shard_map(
        per_device, mesh=mesh, in_specs=in_specs, out_specs=out_specs, check_vma=False
    )
```

profile of v0, /device:TPU:0, one launch (start us, length us, event | category | flops | bytes accessed | tf_op | source)
XLA Modules:
  0.0 419.2 jit_solution(7549125081553769152)
XLA Ops:
  7.2 0.0 all-gather.3.cloned.1.call-start
  7.2 0.7 all-gather.3.cloned.1.call-update
  7.9 0.0 all-reduce.3.cloned.1.call-start
  7.9 78.3 %all-gather.3.cloned.1.call-done = bf16[1,512,4096]{2,1,0:T(8,128)(2,1)} async-done(((bf16[1,64,4096]{2,1,0:T(8,128)(2,1)}), bf16[1,512,4096]{2,1,0:T(8,128)(2,1)}) %all-gather.3.cloned.1.call-update) | async-done | bytes 4194320 | tf_op jit(solution)/shard_map/all_gather | solution.py:11
  86.3 10.5 %fusion.8 = f32[512,1024]{1,0:T(8,128)} fusion(bf16[1,4096,1024]{2,1,0:T(8,128)(2,1)} %param.6, bf16[1,512,4096]{2,1,0:T(8,128)(2,1)} %all-gather.3.cloned.1.call-done), kind=kOutput, calls=%fused_computation.10 | convolution fusion | flops 4294967296 | bytes 14680064 | tf_op jit(solution)/shard_map/dot_general | solution.py:15
  96.7 0.0 copy-start.1
  96.7 0.0 all-reduce.3.cloned.1.call-update
  96.7 0.0 reduce-scatter.2.cloned.1.call-start
  96.8 19.6 %all-reduce.3.cloned.1.call-done = f32[512,1024]{1,0:T(8,128)} async-done(((f32[512,1024]{1,0:T(8,128)}), f32[512,1024]{1,0:T(8,128)}) %all-reduce.3.cloned.1.call-update) | async-done | bytes 2097168 | tf_op jit(solution)/shard_map/psum | solution.py:17
  116.4 0.0 copy-done.1
  116.4 2.9 convert_reduce_fusion
  119.2 10.1 %fusion.10 = f32[4096,512]{0,1:T(8,128)} fusion(bf16[512,1024]{1,0:T(8,128)(2,1)S(1)} %get-tuple-element.9, bf16[1,1024,4096]{2,1,0:T(8,128)(2,1)} %param.8), kind=kOutput, calls=%fused_computation.13 | convolution fusion | flops 4294967296 | bytes 17825792 | tf_op jit(solution)/shard_map/dot_general | solution.py:24
  129.3 0.0 copy-start.2
  129.3 0.0 reduce-scatter.2.cloned.1.call-update
  129.4 0.0 all-gather.5.cloned.1.call-start
  129.4 150.7 %reduce-scatter.2.cloned.1.call-done = f32[512,512]{0,1:T(8,128)} async-done(((f32[4096,512]{0,1:T(8,128)}), f32[512,512]{0,1:T(8,128)}) %reduce-scatter.2.cloned.1.call-update) | async-done | bytes 1048592 | tf_op jit(solution)/shard_map/reduce_scatter | solution.py:23
  280.1 0.0 copy-done.2
  280.1 2.9 fusion.19
  283.0 0.0 all-gather.5.cloned.1.call-update
  283.1 0.2 all-reduce.5.cloned.1.call-start
  283.3 74.0 %all-gather.5.cloned.1.call-done = bf16[4096,512]{0,1:T(8,128)(2,1)} async-done(((bf16[512,512]{0,1:T(8,128)(2,1)}), bf16[4096,512]{0,1:T(8,128)(2,1)}) %all-gather.5.cloned.1.call-update) | async-done | bytes 4194320 | tf_op jit(solution)/shard_map/all_gather | solution.py:36
  357.2 10.5 %fusion.4 = f32[512,1024]{1,0:T(8,128)} fusion(bf16[4096,512]{0,1:T(8,128)(2,1)} %all-gather.5.cloned.1.call-done, bf16[1,1024,4096]{2,1,0:T(8,128)(2,1)} %param.8), kind=kOutput, calls=%fused_computation.6 | convolution fusion | flops 4294967296 | bytes 14680064 | tf_op jit(solution)/shard_map/dot_general | solution.py:37
  367.7 0.0 all-reduce.5.cloned.1.call-update
  367.8 5.1 %fusion = f32[1024]{0:T(1024)S(1)} fusion(bf16[1,1024,4096]{2,1,0:T(8,128)(2,1)} %param.8), kind=kLoop, calls=%fused_computation.2 | loop fusion | flops 12581888 | bytes 8392704 | tf_op jit(solution)/shard_map/reduce_sum | solution.py:16
  372.9 2.5 psum.23
  375.3 0.0 copy-start
  375.3 11.0 %fusion.3 = bf16[1,1024,4096]{2,1,0:T(8,128)(2,1)} fusion(bf16[1,1024,4096]{2,1,0:T(8,128)(2,1)} %param.8, f32[1024]{0:T(1024)S(1)} %get-tuple-element.12, bf16[512,1024]{1,0:T(8,128)(2,1)S(1)} %get-tuple-element.9, bf16[4096,512]{0,1:T(8,128)(2,1)} %all-gather.5.cloned.1.call-done), kind=kOutput, calls=%fused_computation.5 | convolution fusion | flops 4311744512 | bytes 22024192 | tf_op jit(solution)/shard_map/dot_general | solution.py:41
  386.3 1.0 all-reduce.5.cloned.1.call-done
  387.3 0.0 copy-done
  387.3 10.7 %convert_bitcast_fusion = bf16[1,4096,1024]{1,2,0:T(8,128)(2,1)} fusion(bf16[1,512,4096]{2,1,0:T(8,128)(2,1)} %all-gather.3.cloned.1.call-done, f32[512,1024]{1,0:T(8,128)} %all-reduce.5.cloned.1.call-done, f32[512,1024]{1,0:T(8,128)S(1)} %copy-done, f32[1024]{0:T(1024)S(1)} %broadcast_multiply_fusion, f32[1024]{0:T(1024)S(1)} %copy-done.1), kind=kOutput, calls=%fused_computation.12 | convolution fusion | flops 4302831616 | bytes 16785408 | tf_op jit(solution)/shard_map/dot_general | solution.py:53
  398.0 11.9 %copy.9 = bf16[1,4096,1024]{2,1,0:T(8,128)(2,1)} copy(bf16[1,4096,1024]{1,2,0:T(8,128)(2,1)} %convert_bitcast_fusion) | data formatting | bytes 16777216
  410.0 2.7 fusion.21
  (2 shorter events, 0.0 us)
Async XLA Ops:
  7.2 79.1 %all-gather.3.cloned.1.call-start = ((), (), s32[]{:S(2)}) async-start(), calls=%async_computation.1 | async-start | bytes 4718592 | tf_op jit(solution)/shard_map/all_gather | solution.py:11
  7.9 108.5 %all-reduce.3.cloned.1.call-start = ((), (), s32[]{:S(2)}) async-start(), calls=%async_computation.2 | async-start | bytes 4194304 | tf_op jit(solution)/shard_map/psum | solution.py:17
  96.7 19.7 %copy-start.1 = (f32[1024]{0:T(1024)S(1)}, f32[1024]{0:T(1024)}, u32[]{:S(2)}) copy-start(f32[1024]{0:T(1024)} %param.7) | copy-start | bytes 12292
  96.7 183.3 %reduce-scatter.2.cloned.1.call-start = ((), (), s32[]{:S(2)}) async-start(), calls=%async_computation.3 | async-start | bytes 9437184 | tf_op jit(solution)/shard_map/reduce_scatter | solution.py:23
  129.3 150.7 %copy-start.2 = (f32[1,512]{1,0:T(1,128)S(1)}, f32[1,512]{1,0:T(1,128)}, u32[]{:S(2)}) copy-start(f32[1,512]{1,0:T(1,128)} %param.9) | copy-start | bytes 6148
  129.4 227.9 %all-gather.5.cloned.1.call-start = ((), (), s32[]{:S(2)}) async-start(), calls=%async_computation.4 | async-start | bytes 4718592 | tf_op jit(solution)/shard_map/all_gather | solution.py:36
  283.1 104.3 %all-reduce.5.cloned.1.call-start = ((), (), s32[]{:S(2)}) async-start(), calls=%async_computation.5 | async-start | bytes 4194304 | tf_op jit(solution)/shard_map/psum | solution.py:40
  375.3 12.0 %copy-start = (f32[512,1024]{1,0:T(8,128)S(1)}, f32[512,1024]{1,0:T(8,128)}, u32[]{:S(2)}) copy-start(f32[512,1024]{1,0:T(8,128)} %all-reduce.3.cloned.1.call-done) | copy-start | bytes 6291460
Sparse Core Ops, SparseCore 0:
  10.1 76.0 all-gather.2
  96.9 19.4 all-reduce.2
  129.5 150.5 reduce-scatter.1
  283.2 74.0 all-gather.4
  367.9 19.4 all-reduce.4
where the time goes:
time: 420 us; the launch traced here: 419 us
  waiting for transfers between devices  324 us (77%)
  matrix products  52.7 us (13%)
  between operations  13.8 us (3%)
  other arithmetic  13.6 us (3%)
  local copies, waits for them, and re-layouts  11.9 us (3%)
    reduce_scatter x1, waiting for transfers between devices, per_device(): lax.psum_scatter(lax.dot_general(decoder, features, (((0,), (1,)), ((), (...  151 us
    all_gather x1, waiting for transfers between devices, per_device(): gathered = lax.all_gather(streams, 'lat', axis=1, tiled=True)  78.3 us
    all_gather x1, waiting for transfers between devices, per_device(): err_full = lax.all_gather(err_round, 'lat', axis=0, tiled=True)  74 us
    psum x1, waiting for transfers between devices, per_device(): pre_sum, strength = lax.psum((pre_part, row_norm), 'layer')  19.6 us
    unnamed x7, local copies, waits for them, and re-layouts  11.9 us
    dot_general x1, matrix products, per_device(): lax.dot_general(features, err_full, (((0,), (1,)), ((), ())), preferred_e...  11 us
    dot_general x1, matrix products, per_device(): lax.dot_general(inputs_full, pre_round, (((0,), (0,)), ((), ())), preferr...  10.7 us
    dot_general x1, matrix products, per_device(): lax.dot_general(err_full, decoder, (((0,), (1,)), ((), ())), preferred_el...  10.5 us
  transfers between devices with their start and end apart: 5, of which 5 were waited for; matrix products, arithmetic and copies ran while one was open for 4% of the time, Pallas kernels for 0%

commit v1 on v0

v1 whole, which is shorter than its diff:
```python
import functools

import jax
import jax.numpy as jnp
from jax import lax
from jax.experimental import pallas as pl
from jax.experimental.pallas import tpu as pltpu
from jax.sharding import PartitionSpec as P

penalty_weight = 1.0
epsilon_sq = 1e-06
MESH = pl.DeviceIdType.MESH
MIB = 1024 * 1024
F32 = jnp.float32
BF16 = jnp.bfloat16


def ring_neighbours(n):
    index = lax.axis_index("lat")
    if n != 8:
        return lax.rem(index + 1, n), lax.rem(index + n - 1, n)
    half = n // 2

    def place_of(i):
        z, y = i // 2, lax.rem(i, 2)
        return jnp.where(y == 0, z, n - 1 - z)

    def index_of(p):
        return jnp.where(p < half, 2 * p, 2 * (n - 1 - p) + 1)

    place = place_of(index)
    return index_of(lax.rem(place + 1, n)), index_of(lax.rem(place + n - 1, n))


def step_kernel(
    n, x_ref, enc_hbm, enc_bias_ref, dec_hbm, dec_bias_ref, norm_ref,
    full_out, feat_out, err_out, round_out, bias_grad_ref, dec_bias_grad_ref,
    enc, dec, full, part, part_in, pre, feat, partial, sum_right, sum_left, in_right, in_left,
    err, grad, grad_in, rounded, norm_in,
    g_send, g_recv, r_send, r_recv, e_send, e_recv, p_send, p_recv, q_send, q_recv, n_sem, w_sem, o_sem,
):
    rows, width = x_ref.shape
    latents = enc.shape[1]
    half = n // 2
    hw = width // 2
    total = n * rows
    scale = float(1.0 / (total ** 0.5))
    right, left = ring_neighbours(n)
    other = 1 - lax.axis_index("layer")
    lat = lax.axis_index("lat")
    to_right, to_left, to_other = {"lat": right}, {"lat": left}, {"layer": other}
    sending = []

    load_enc = pltpu.make_async_copy(enc_hbm, enc, w_sem.at[0])
    load_dec = pltpu.make_async_copy(dec_hbm, dec, w_sem.at[1])
    load_enc.start()
    load_dec.start()

    barrier = pltpu.get_barrier_semaphore()
    for target in (to_right, to_left, to_other):
        pl.semaphore_signal(barrier, inc=1, device_id=target, device_id_type=MESH)

    def slot_rows(slot, count=1):
        return pl.ds(slot * rows, count * rows)

    def send(src, dst, s_sem, r_sem, target):
        copy = pltpu.make_async_remote_copy(
            src_ref=src, dst_ref=dst, send_sem=s_sem, recv_sem=r_sem,
            device_id=target, device_id_type=MESH,
        )
        copy.start()
        sending.append(copy)
        return copy

    def step_span(d):
        if d == 0:
            return 0, 1
        if d == half:
            return n - 1, 1
        return 2 * d - 1, 2

    def gather(buf, s_sem, r_sem, consume):
        got = {}

        def forward(d, h, way):
            if d > half or (d == half and h != way):
                return
            if way == 0:
                src = 0 if d == 1 else 2 * d - 3
                dst = n - 1 if d == half else 2 * d - 1
            else:
                src = 2 * (d - 1)
                dst = n - 1 if d == half else 2 * d
            cols = pl.ds(h * hw, hw)
            got[(d, h, way)] = send(
                buf.at[slot_rows(src), cols], buf.at[slot_rows(dst), cols],
                s_sem.at[way, d - 1, h], r_sem.at[way, d - 1, h],
                to_right if way == 0 else to_left,
            )

        for order in range(2):
            for way in range(2):
                forward(1, (order + way) % 2, way)
        consume(0)
        for d in range(1, half + 1):
            for order in range(2):
                for way in range(2):
                    h = (order + way) % 2
                    if (d, h, way) in got:
                        got[(d, h, way)].wait_recv()
                        forward(d + 1, h, way)
            consume(d)

    full[slot_rows(0), :] = x_ref[...]
    pl.semaphore_wait(barrier, 3)
    swap_norm = send(norm_ref, norm_in, n_sem.at[0], n_sem.at[1], to_other)

    tile = min(256, latents)
    swaps = {}

    def finish_pre(d):
        slot, count = step_span(d)
        swaps[d].wait_recv()

        @pl.loop(0, count * rows // 16)
        def _(i):
            r = pl.ds(pl.multiple_of(slot * rows + i * 16, 16), 16)
            value = part[r, :] + part_in[r, :] + enc_bias_ref[...]
            pre[r, :] = value
            soft = jnp.maximum(value, 0.0) + jnp.log1p(jnp.exp(-jnp.abs(value)))
            feat[r, :] = soft.astype(BF16)

    def encode(d):
        if d == 0:
            load_enc.wait()
        slot, count = step_span(d)
        r = slot_rows(slot, count)

        @pl.loop(0, latents // tile)
        def _(j):
            c = pl.ds(pl.multiple_of(j * tile, tile), tile)
            part[r, c] = jnp.dot(full[r, :], enc[:, c], preferred_element_type=F32)

        swaps[d] = send(part.at[r, :], part_in.at[r, :], p_send.at[d], p_recv.at[d], to_other)
        if d >= 1:
            finish_pre(d - 1)

    gather(full, g_send, g_recv, encode)
    save_full = pltpu.make_async_copy(full, full_out, o_sem.at[0])
    save_full.start()
    finish_pre(half)
    save_feat = pltpu.make_async_copy(feat, feat_out, o_sem.at[1])
    save_feat.start()

    load_dec.wait()
    wide = min(512, width)
    own = width // n

    def decode(d):
        slot, count = step_span(d)
        r = slot_rows(slot, count)
        to = pl.ds(0, count * rows)

        @pl.loop(0, width // wide)
        def _(j):
            c = pl.ds(pl.multiple_of(j * wide, wide), wide)
            partial[to, c] = jnp.dot(feat[r, :], dec[:, c], preferred_element_type=F32)

        mine = pl.ds(pl.multiple_of(lat * own, own), own)
        partial[to, mine] = partial[to, mine] + dec_bias_ref[...]

    def merge(source, base, arrived, index, target, h):
        @pl.loop(0, rows // 16)
        def _(i):
            r = pl.ds(pl.multiple_of(i * 16, 16), 16)
            c = pl.ds(h * hw, hw)
            value = source[pl.ds(pl.multiple_of(base + i * 16, 16), 16), c]
            if arrived is not None:
                value = value + arrived[index, r, c].astype(F32)
            target[r, c] = value.astype(target.dtype)

    moving = {}
    for d in range(half, 0, -1):
        decode(d)
        for order in range(2):
            for way in range(2):
                h = (order + way) % 2
                if d == half and h != way:
                    continue
                base = 0 if d == half or way == 1 else rows
                out = (sum_right, sum_left)[way]
                arrive = (in_right, in_left)[way]
                before = moving.get((d + 1, h, way))
                if before is not None:
                    before.wait_recv()
                merge(partial, base, None if before is None else arrive, d, out.at[d - 1], h)
                c = pl.ds(h * hw, hw)
                moving[(d, h, way)] = send(
                    out.at[d - 1, :, c], arrive.at[d - 1, :, c],
                    r_send.at[way, d - 1, h], r_recv.at[way, d - 1, h],
                    to_right if way == 0 else to_left,
                )
    decode(0)
    for order in range(2):
        for way in range(2):
            moving[(1, (order + way) % 2, way)].wait_recv()

    @pl.loop(0, rows // 16)
    def _(i):
        r = pl.ds(pl.multiple_of(i * 16, 16), 16)
        for h in range(2):
            c = pl.ds(h * hw, hw)
            recon = partial[r, c] + in_right[0, r, c].astype(F32) + in_left[0, r, c].astype(F32)
            err[r, c] = ((recon - x_ref[r, c].astype(F32)) * scale).astype(BF16)

    swap_norm.wait_recv()
    bias_grad_ref[...] = jnp.zeros_like(bias_grad_ref)
    grad_swaps = {}

    def finish_grad(d):
        slot, count = step_span(d)
        grad_swaps[d].wait_recv()

        @pl.loop(0, count * rows // 16)
        def _(i):
            r = pl.ds(pl.multiple_of(slot * rows + i * 16, 16), 16)
            strength = norm_ref[0:1, :] + norm_in[0:1, :]
            value = grad[r, :] + grad_in[r, :] + (penalty_weight * scale) * strength
            value = value * jax.nn.sigmoid(pre[r, :])
            rounded[r, :] = value.astype(BF16)
            bias_grad_ref[...] += jnp.sum(value, axis=0, keepdims=True)

    def decode_grad(d):
        slot, count = step_span(d)
        r = slot_rows(slot, count)

        @pl.loop(0, latents // tile)
        def _(j):
            c = pl.ds(pl.multiple_of(j * tile, tile), tile)
            grad[r, c] = lax.dot_general(
                err[r, :], dec[c, :], (((1,), (1,)), ((), ())), preferred_element_type=F32
            )

        grad_swaps[d] = send(grad.at[r, :], grad_in.at[r, :], q_send.at[d], q_recv.at[d], to_other)
        if d >= 1:
            finish_grad(d - 1)

    gather(err, e_send, e_recv, decode_grad)
    save_err = pltpu.make_async_copy(err, err_out, o_sem.at[2])
    save_err.start()
    mine = pl.ds(pl.multiple_of(lat * own, own), own)
    dec_bias_grad_ref[...] = jnp.zeros_like(dec_bias_grad_ref)

    @pl.loop(0, total // 64)
    def _(i):
        r = pl.ds(pl.multiple_of(i * 64, 64), 64)
        dec_bias_grad_ref[...] += jnp.sum(err[r, mine].astype(F32), axis=0, keepdims=True)

    finish_grad(half)
    save_round = pltpu.make_async_copy(rounded, round_out, o_sem.at[3])
    save_round.start()
    for copy in sending:
        copy.wait_send()
    for save in (save_full, save_feat, save_err, save_round):
        save.wait()


def main_call(n, x, enc, enc_bias, dec, dec_bias, norm):
    rows, width = x.shape
    latents = enc.shape[1]
    total = n * rows
    half = n // 2
    vmem = pl.BlockSpec(memory_space=pltpu.VMEM)
    hbm = pl.BlockSpec(memory_space=pl.ANY)
    dma = pltpu.SemaphoreType.DMA
    steps = dma((2, half, 2))
    swap = dma((half + 1,))
    return pl.pallas_call(
        functools.partial(step_kernel, n),
        out_shape=(
            jax.ShapeDtypeStruct((total, width), BF16),
            jax.ShapeDtypeStruct((total, latents), BF16),
            jax.ShapeDtypeStruct((total, width), BF16),
            jax.ShapeDtypeStruct((total, latents), BF16),
            jax.ShapeDtypeStruct((1, latents), F32),
            jax.ShapeDtypeStruct((1, width // n), F32),
        ),
        in_specs=[vmem, hbm, vmem, hbm, vmem, vmem],
        out_specs=(hbm, hbm, hbm, hbm, vmem, vmem),
        scratch_shapes=[
            pltpu.VMEM((width, latents), BF16),
            pltpu.VMEM((latents, width), BF16),
            pltpu.VMEM((total, width), BF16),
            pltpu.VMEM((total, latents), F32),
            pltpu.VMEM((total, latents), F32),
            pltpu.VMEM((total, latents), F32),
            pltpu.VMEM((total, latents), BF16),
            pltpu.VMEM((2 * rows, width), F32),
            pltpu.VMEM((half, rows, width), BF16),
            pltpu.VMEM((half, rows, width), BF16),
            pltpu.VMEM((half, rows, width), BF16),
            pltpu.VMEM((half, rows, width), BF16),
            pltpu.VMEM((total, width), BF16),
            pltpu.VMEM((total, latents), F32),
            pltpu.VMEM((total, latents), F32),
            pltpu.VMEM((total, latents), BF16),
            pltpu.VMEM((8, latents), F32),
            steps, steps, steps, steps, steps, steps, swap, swap, swap, swap,
            dma((2,)), dma((2,)), dma((4,)),
        ],
        compiler_params=pltpu.CompilerParams(
            collective_id=0, has_side_effects=True, vmem_limit_bytes=60 * MIB
        ),
        cost_estimate=pl.CostEstimate(
            flops=6 * total * width * latents, bytes_accessed=32 * MIB, transcendentals=0
        ),
    )(x, enc, enc_bias, dec, dec_bias, norm)


def enc_grad_kernel(full_ref, round_ref, out_ref):
    out_ref[...] = lax.dot_general(
        full_ref[...], round_ref[...], (((0,), (0,)), ((), ())), preferred_element_type=F32
    ).astype(BF16)


def enc_grad_call(full, rounded):
    total, width = full.shape
    latents = rounded.shape[1]
    tile = 512
    return pl.pallas_call(
        enc_grad_kernel,
        grid=(width // tile,),
        out_shape=jax.ShapeDtypeStruct((width, latents), BF16),
        in_specs=[
            pl.BlockSpec((total, tile), lambda i: (0, i)),
            pl.BlockSpec((total, latents), lambda i: (0, 0)),
        ],
        out_specs=pl.BlockSpec((tile, latents), lambda i: (i, 0)),
        compiler_params=pltpu.CompilerParams(vmem_limit_bytes=40 * MIB),
        cost_estimate=pl.CostEstimate(
            flops=2 * total * width * latents, bytes_accessed=13 * MIB, transcendentals=0
        ),
    )(full, rounded)


def dec_grad_kernel(scale, feat_ref, err_ref, dec_ref, norm_ref, out_ref):
    total, width = err_ref.shape
    chunk = 512
    feats = feat_ref[...].T
    sums = jnp.dot(feats, jnp.ones((total, 128), BF16), preferred_element_type=F32)[:, :1]
    factor = penalty_weight * scale * sums / norm_ref[...]
    for j in range(width // chunk):
        c = pl.ds(j * chunk, chunk)
        direct = jnp.dot(feats, err_ref[:, c], preferred_element_type=F32)
        out_ref[:, c] = (direct + factor * dec_ref[:, c].astype(F32)).astype(BF16)


def dec_grad_call(feat, err, dec, norm):
    total, width = err.shape
    latents = feat.shape[1]
    tile = 256
    scale = float(1.0 / (total ** 0.5))
    return pl.pallas_call(
        functools.partial(dec_grad_kernel, scale),
        grid=(latents // tile,),
        out_shape=jax.ShapeDtypeStruct((latents, width), BF16),
        in_specs=[
            pl.BlockSpec((total, tile), lambda i: (0, i)),
            pl.BlockSpec((total, width), lambda i: (0, 0)),
            pl.BlockSpec((tile, width), lambda i: (i, 0)),
            pl.BlockSpec((tile, 1), lambda i: (i, 0)),
        ],
        out_specs=pl.BlockSpec((tile, width), lambda i: (i, 0)),
        compiler_params=pltpu.CompilerParams(vmem_limit_bytes=40 * MIB),
        cost_estimate=pl.CostEstimate(
            flops=2 * total * width * latents, bytes_accessed=21 * MIB, transcendentals=0
        ),
    )(feat, err, dec, norm)


def per_device(n, streams, enc_weight, enc_bias, dec_weight, dec_bias):
    decoder = dec_weight[0]
    row_norm = jnp.sqrt(jnp.sum(jnp.square(decoder.astype(F32)), axis=1) + epsilon_sq)
    norm_rows = jnp.broadcast_to(row_norm[None, :], (8, row_norm.shape[0]))
    full, feat, err, rounded, enc_bias_grad, dec_bias_grad = main_call(
        n, streams[0], enc_weight[0], enc_bias[None, :], decoder, dec_bias, norm_rows
    )
    dec_grad = dec_grad_call(feat, err, decoder, row_norm[:, None])
    enc_grad = enc_grad_call(full, rounded)
    return (enc_grad[None], enc_bias_grad[0], dec_grad[None], dec_bias_grad)


def solution(mesh):
    in_specs = (
        P("layer", ("groups", "lat"), None),
        P(("groups", "layer"), None, "lat"),
        P(("groups", "lat")),
        P(("groups", "layer"), "lat", None),
        P(("groups", "layer"), "lat"),
    )
    out_specs = (
        P(("groups", "layer"), None, "lat"),
        P(("groups", "lat")),
        P(("groups", "layer"), "lat", None),
        P(("groups", "layer"), "lat"),
    )
    return jax.shard_map(
        functools.partial(per_device, mesh.shape["lat"]), mesh=mesh,
        in_specs=in_specs, out_specs=out_specs, check_vma=False,
    )
```

time: 420 us -> 173 us (0.41)
  waiting for transfers between devices: 324 us -> 0 us
  Pallas kernels: 0 us -> 159 us
  matrix products: 52.7 us -> 0 us
  between operations: 13.8 us -> 0.67 us
  other arithmetic: 13.6 us -> 5.08 us
    pallas_call x0 -> x3, Pallas kernels: none -> 159 us  [the longest x1 144 us: main_call(): pl.pallas_call(functools.partial(step_kernel, n), out_shape=(jax.ShapeDty...]
    all_gather x2 -> x0, waiting for transfers between devices: 152 us -> none  [the longest x1 78.3 us: per_device(): gathered = lax.all_gather(streams, 'lat', axis=1, tiled=True)]
    reduce_scatter x1 -> x0, waiting for transfers between devices: 151 us -> none  [per_device(): lax.psum_scatter(lax.dot_general(decoder, features, (((0,), (1,)), ((), (...]
    dot_general x5 -> x0, matrix products: 52.7 us -> none  [the longest x1 11 us: per_device(): lax.dot_general(features, err_full, (((0,), (1,)), ((), ())), preferred_e...]
    psum x2 -> x0, waiting for transfers between devices: 20.6 us -> none  [the longest x1 19.6 us: per_device(): pre_sum, strength = lax.psum((pre_part, row_norm), 'layer')]
    reduce_sum x4 -> x1, other arithmetic: 13.6 us -> 5.07 us  [per_device(): jnp.sum(jnp.square(decoder.astype(F32)), axis=1) + epsilon_sq]
    unnamed x7 -> x16, local copies, waits for them, and re-layouts: 11.9 us -> 7.98 us
  transfers between devices with their start and end apart: 5 -> 0, of which waited for: 5 -> 0; matrix products, arithmetic and copies ran while one was open for 4% -> 0% of each run, Pallas kernels for 0% -> 0%
where the time goes in v1:
time: 173 us
  Pallas kernels  159 us (92%)
  local copies, waits for them, and re-layouts  8.82 us (5%)
  other arithmetic  5.08 us (3%)
    pallas_call x1, Pallas kernels, main_call(): pl.pallas_call(functools.partial(step_kernel, n), out_shape=(jax.ShapeDty...  144 us
    unnamed x16, local copies, waits for them, and re-layouts  7.98 us
    pallas_call x1, Pallas kernels, enc_grad_call(): pl.pallas_call(enc_grad_kernel, grid=(width // tile,), out_shape=jax.Shap...  7.82 us
    pallas_call x1, Pallas kernels, dec_grad_call(): pl.pallas_call(functools.partial(dec_grad_kernel, scale), grid=(latents /...  7.06 us
    reduce_sum x1, other arithmetic, per_device(): jnp.sum(jnp.square(decoder.astype(F32)), axis=1) + epsilon_sq  5.07 us

profile of v1, /device:TPU:0, one launch (start us, length us, event | category | flops | bytes accessed | tf_op | source)
XLA Modules:
  0.0 173.1 jit_solution(1321728639005316857)
XLA Ops:
  0.6 5.1 %multiply_reduce_fusion = f32[1024]{0:T(1024)S(1)} fusion(bf16[1,1024,4096]{2,1,0:T(8,128)(2,1)} %param.8), kind=kLoop, calls=%fused_computation | loop fusion | flops 12581888 | bytes 8392704 | tf_op jit(solution)/shard_map/reduce_sum | solution.py:383
  5.7 0.6 broadcast_in_dim.17.norm_ref
  6.3 143.7 %shard_map.84 = (bf16[512,4096]{1,0:T(8,128)(2,1)}, bf16[512,1024]{1,0:T(8,128)(2,1)}, bf16[512,4096]{1,0:T(8,128)(2,1)}, bf16[512,1024]{1,0:T(8,128)(2,1)}, f32[1,1024]{1,0:T(1,128)}, /*index=5*/f32[1,512]{1,0:T(1,128)}) custom-call(bf16[64,4096]{1,0:T(8,128)(2,1)} %bitcast.15, bf16[4096,1024]{1,0:T(8,128)(2,1)} %bitcast.14, f32[1,1024]{1,0:T(1,128)} %bitcast.16, ...), custom_call_target="tpu_custom_call" | custom-call | flops 12884901888 | bytes 33554432 | tf_op jit(solution)/shard_map/pallas_call | solution.py:278
  150.0 0.2 copy.9.norm_ref
  150.3 0.0 copy-start
  150.3 3.4 %copy-done = bf16[1,1024,4096]{2,1,0:T(8,128)(2,1)S(1)} copy-done((bf16[1,1024,4096]{2,1,0:T(8,128)(2,1)S(1)}, bf16[1,1024,4096]{2,1,0:T(8,128)(2,1)}, u32[]{:S(2)}) %copy-start) | copy-done | bytes 8388632
  153.6 0.0 copy-start.1
  153.6 2.2 %copy-done.1 = bf16[512,4096]{1,0:T(8,128)(2,1)S(1)} copy-done((bf16[512,4096]{1,0:T(8,128)(2,1)S(1)}, bf16[512,4096]{1,0:T(8,128)(2,1)}, u32[]{:S(2)}) %copy-start.1) | copy-done | bytes 4194328
  155.8 0.0 copy-start.2
  155.8 1.2 copy-done.2
  157.1 0.0 copy-start.3
  157.1 0.0 copy-start.4
  157.1 7.1 %shard_map.86 = bf16[1024,4096]{1,0:T(8,128)(2,1)} custom-call(bf16[512,1024]{1,0:T(8,128)(2,1)S(1)} %copy-done.2, bf16[512,4096]{1,0:T(8,128)(2,1)S(1)} %copy-done.1, bf16[1024,4096]{1,0:T(8,128)(2,1)S(1)} %bitcast.10, f32[1024,1]{1,0:T(8,128)S(1)} %copy.9.norm_ref), custom_call_target="tpu_custom_call" | custom-call | flops 4294967296 | bytes 22020096 | tf_op jit(solution)/shard_map/pallas_call | solution.py:363
  164.1 0.0 copy-start.5
  164.1 0.0 copy-start.6
  164.1 0.0 copy-done.3
  164.1 0.0 copy-done.4
  164.1 7.8 %shard_map.85 = bf16[4096,1024]{1,0:T(8,128)(2,1)} custom-call(bf16[512,4096]{1,0:T(8,128)(2,1)S(1)} %copy-done.3, bf16[512,1024]{1,0:T(8,128)(2,1)S(1)} %copy-done.4), custom_call_target="tpu_custom_call" | custom-call | flops 4294967296 | bytes 13631488 | tf_op jit(solution)/shard_map/pallas_call | solution.py:330
  171.9 0.0 copy-done.5
  172.0 0.6 copy.12
  172.5 0.0 copy-done.6
  172.5 0.6 copy.13
  (1 shorter events, 0.0 us)
Async XLA Ops:
  150.3 3.4 %copy-start = (bf16[1,1024,4096]{2,1,0:T(8,128)(2,1)S(1)}, bf16[1,1024,4096]{2,1,0:T(8,128)(2,1)}, u32[]{:S(2)}) copy-start(bf16[1,1024,4096]{2,1,0:T(8,128)(2,1)} %param.8) | copy-start | bytes 25165828
  153.6 2.2 %copy-start.1 = (bf16[512,4096]{1,0:T(8,128)(2,1)S(1)}, bf16[512,4096]{1,0:T(8,128)(2,1)}, u32[]{:S(2)}) copy-start(bf16[512,4096]{1,0:T(8,128)(2,1)} %get-tuple-element.14.err_ref) | copy-start | bytes 12582916
  155.8 1.2 copy-start.2
  157.1 7.1 %copy-start.3 = (bf16[512,4096]{1,0:T(8,128)(2,1)S(1)}, bf16[512,4096]{1,0:T(8,128)(2,1)}, u32[]{:S(2)}) copy-start(bf16[512,4096]{1,0:T(8,128)(2,1)} %get-tuple-element.10.full_ref) | copy-start | bytes 12582916
  157.1 7.1 %copy-start.4 = (bf16[512,1024]{1,0:T(8,128)(2,1)S(1)}, bf16[512,1024]{1,0:T(8,128)(2,1)}, u32[]{:S(2)}) copy-start(bf16[512,1024]{1,0:T(8,128)(2,1)} %get-tuple-element.11.round_ref) | copy-start | bytes 3145732
  164.1 7.8 %copy-start.5 = (f32[1,1024]{1,0:T(1,128)S(1)}, f32[1,1024]{1,0:T(1,128)}, u32[]{:S(2)}) copy-start(f32[1,1024]{1,0:T(1,128)} %get-tuple-element.12) | copy-start | bytes 12292
  164.1 8.4 %copy-start.6 = (f32[1,512]{1,0:T(1,128)S(1)}, f32[1,512]{1,0:T(1,128)}, u32[]{:S(2)}) copy-start(f32[1,512]{1,0:T(1,128)} %get-tuple-element.23) | copy-start | bytes 6148

commit v2 on v1

--- a/solution.py
+++ b/solution.py
@@ -33,10 +33,10 @@
 
 
 def step_kernel(
-    n, x_ref, enc_hbm, enc_bias_ref, dec_hbm, dec_bias_ref, norm_ref,
-    full_out, feat_out, err_out, round_out, bias_grad_ref, dec_bias_grad_ref,
+    n, x_ref, enc_hbm, enc_bias_ref, dec_hbm, dec_bias_ref,
+    full_out, feat_out, err_out, round_out, norm_ref, bias_grad_ref, dec_bias_grad_ref,
     enc, dec, full, part, part_in, pre, feat, partial, sum_right, sum_left, in_right, in_left,
-    err, grad, grad_in, rounded, norm_in,
+    err, grad, grad_in, rounded, norm_row, norm_in,
     g_send, g_recv, r_send, r_recv, e_send, e_recv, p_send, p_recv, q_send, q_recv, n_sem, w_sem, o_sem,
 ):
     rows, width = x_ref.shape
@@ -113,7 +113,6 @@
 
     full[slot_rows(0), :] = x_ref[...]
     pl.semaphore_wait(barrier, 3)
-    swap_norm = send(norm_ref, norm_in, n_sem.at[0], n_sem.at[1], to_other)
 
     tile = min(256, latents)
     swaps = {}
@@ -130,6 +129,23 @@
             soft = jnp.maximum(value, 0.0) + jnp.log1p(jnp.exp(-jnp.abs(value)))
             feat[r, :] = soft.astype(BF16)
 
+    norm_swap = []
+
+    def norms():
+        load_dec.wait()
+
+        @pl.loop(0, latents // 16)
+        def _(i):
+            r = pl.ds(pl.multiple_of(i * 16, 16), 16)
+            value = jnp.square(dec[r, :].astype(F32))
+            value = jnp.sqrt(jnp.sum(value, axis=1, keepdims=True) + epsilon_sq)
+            norm_ref[r, :] = jnp.broadcast_to(value, (16, 128))
+
+        for i in range(latents // 128):
+            r = pl.ds(i * 128, 128)
+            norm_row[:, r] = norm_ref[r, :].T[:8, :]
+        norm_swap.append(send(norm_row, norm_in, n_sem.at[0], n_sem.at[1], to_other))
+
     def encode(d):
         if d == 0:
             load_enc.wait()
@@ -144,6 +160,8 @@
         swaps[d] = send(part.at[r, :], part_in.at[r, :], p_send.at[d], p_recv.at[d], to_other)
         if d >= 1:
             finish_pre(d - 1)
+        if d == 1:
+            norms()
 
     gather(full, g_send, g_recv, encode)
     save_full = pltpu.make_async_copy(full, full_out, o_sem.at[0])
@@ -152,7 +170,6 @@
     save_feat = pltpu.make_async_copy(feat, feat_out, o_sem.at[1])
     save_feat.start()
 
-    load_dec.wait()
     wide = min(512, width)
     own = width // n
 
@@ -213,7 +230,7 @@
             recon = partial[r, c] + in_right[0, r, c].astype(F32) + in_left[0, r, c].astype(F32)
             err[r, c] = ((recon - x_ref[r, c].astype(F32)) * scale).astype(BF16)
 
-    swap_norm.wait_recv()
+    norm_swap[0].wait_recv()
     bias_grad_ref[...] = jnp.zeros_like(bias_grad_ref)
     grad_swaps = {}
 
@@ -224,7 +241,7 @@
         @pl.loop(0, count * rows // 16)
         def _(i):
             r = pl.ds(pl.multiple_of(slot * rows + i * 16, 16), 16)
-            strength = norm_ref[0:1, :] + norm_in[0:1, :]
+            strength = norm_row[0:1, :] + norm_in[0:1, :]
             value = grad[r, :] + grad_in[r, :] + (penalty_weight * scale) * strength
             value = value * jax.nn.sigmoid(pre[r, :])
             rounded[r, :] = value.astype(BF16)
@@ -265,7 +282,7 @@
         save.wait()
 
 
-def main_call(n, x, enc, enc_bias, dec, dec_bias, norm):
+def main_call(n, x, enc, enc_bias, dec, dec_bias):
     rows, width = x.shape
     latents = enc.shape[1]
     total = n * rows
@@ -282,11 +299,12 @@
             jax.ShapeDtypeStruct((total, latents), BF16),
             jax.ShapeDtypeStruct((total, width), BF16),
             jax.ShapeDtypeStruct((total, latents), BF16),
+            jax.ShapeDtypeStruct((latents, 128), F32),
             jax.ShapeDtypeStruct((1, latents), F32),
             jax.ShapeDtypeStruct((1, width // n), F32),
         ),
-        in_specs=[vmem, hbm, vmem, hbm, vmem, vmem],
-        out_specs=(hbm, hbm, hbm, hbm, vmem, vmem),
+        in_specs=[vmem, hbm, vmem, hbm, vmem],
+        out_specs=(hbm, hbm, hbm, hbm, vmem, vmem, vmem),
         scratch_shapes=[
             pltpu.VMEM((width, latents), BF16),
             pltpu.VMEM((latents, width), BF16),
@@ -305,6 +323,7 @@
             pltpu.VMEM((total, latents), F32),
             pltpu.VMEM((total, latents), BF16),
             pltpu.VMEM((8, latents), F32),
+            pltpu.VMEM((8, latents), F32),
             steps, steps, steps, steps, steps, steps, swap, swap, swap, swap,
             dma((2,)), dma((2,)), dma((4,)),
         ],
@@ -314,80 +333,82 @@
         cost_estimate=pl.CostEstimate(
             flops=6 * total * width * latents, bytes_accessed=32 * MIB, transcendentals=0
         ),
-    )(x, enc, enc_bias, dec, dec_bias, norm)
-
-
-def enc_grad_kernel(full_ref, round_ref, out_ref):
-    out_ref[...] = lax.dot_general(
+    )(x, enc, enc_bias, dec, dec_bias)
+
+
+def weight_grad_kernel(
+    scale, full_ref, round_ref, feat_ref, err_ref, dec_ref, norm_ref, bias_grad_ref, dec_bias_grad_ref,
+    enc_out, dec_out, bias_grad_out, dec_bias_grad_out, feats, factor,
+):
+    total = feat_ref.shape[0]
+    latents, span = dec_ref.shape
+
+    @pl.when(pl.program_id(0) == 0)
+    def _():
+        feats[...] = feat_ref[...].T
+        sums = jnp.dot(feats[...], jnp.ones((total, 128), BF16), preferred_element_type=F32)
+        factor[...] = penalty_weight * scale * sums / norm_ref[...]
+        bias_grad_out[...] = bias_grad_ref[...]
+        dec_bias_grad_out[...] = dec_bias_grad_ref[...]
+
+    enc_out[...] = lax.dot_general(
         full_ref[...], round_ref[...], (((0,), (0,)), ((), ())), preferred_element_type=F32
     ).astype(BF16)
-
-
-def enc_grad_call(full, rounded):
+    step = min(256, latents)
+    for j in range(latents // step):
+        r = pl.ds(j * step, step)
+        direct = jnp.dot(feats[r, :], err_ref[...], preferred_element_type=F32)
+        shrink = factor[r, :1] * dec_ref[r, :].astype(F32)
+        dec_out[r, :] = (direct + shrink).astype(BF16)
+
+
+def weight_grad_call(full, rounded, feat, err, dec, norm, bias_grad, dec_bias_grad):
     total, width = full.shape
     latents = rounded.shape[1]
+    own = dec_bias_grad.shape[1]
     tile = 512
+    scale = float(1.0 / (total ** 0.5))
+
+    def whole(rows, columns):
+        return pl.BlockSpec((rows, columns), lambda i: (0, 0))
+
+    def columns_of(rows):
+        return pl.BlockSpec((rows, tile), lambda i: (0, i))
+
     return pl.pallas_call(
-        enc_grad_kernel,
+        functools.partial(weight_grad_kernel, scale),
         grid=(width // tile,),
-        out_shape=jax.ShapeDtypeStruct((width, latents), BF16),
+        out_shape=(
+            jax.ShapeDtypeStruct((width, latents), BF16),
+            jax.ShapeDtypeStruct((latents, width), BF16),
+            jax.ShapeDtypeStruct((1, latents), F32),
+            jax.ShapeDtypeStruct((1, own), F32),
+        ),
         in_specs=[
-            pl.BlockSpec((total, tile), lambda i: (0, i)),
-            pl.BlockSpec((total, latents), lambda i: (0, 0)),
+            columns_of(total), whole(total, latents), whole(total, latents), columns_of(total),
+            columns_of(latents), whole(latents, 128), whole(1, latents), whole(1, own),
         ],
-        out_specs=pl.BlockSpec((tile, latents), lambda i: (i, 0)),
-        compiler_params=pltpu.CompilerParams(vmem_limit_bytes=40 * MIB),
+        out_specs=(
+            pl.BlockSpec((tile, latents), lambda i: (i, 0)), columns_of(latents),
+            whole(1, latents), whole(1, own),
+        ),
+        scratch_shapes=[pltpu.VMEM((latents, total), BF16), pltpu.VMEM((latents, 128), F32)],
+        compiler_params=pltpu.CompilerParams(vmem_limit_bytes=60 * MIB),
         cost_estimate=pl.CostEstimate(
-            flops=2 * total * width * latents, bytes_accessed=13 * MIB, transcendentals=0
-        ),
-    )(full, rounded)
-
-
-def dec_grad_kernel(scale, feat_ref, err_ref, dec_ref, norm_ref, out_ref):
-    total, width = err_ref.shape
-    chunk = 512
-    feats = feat_ref[...].T
-    sums = jnp.dot(feats, jnp.ones((total, 128), BF16), preferred_element_type=F32)[:, :1]
-    factor = penalty_weight * scale * sums / norm_ref[...]
-    for j in range(width // chunk):
-        c = pl.ds(j * chunk, chunk)
-        direct = jnp.dot(feats, err_ref[:, c], preferred_element_type=F32)
-        out_ref[:, c] = (direct + factor * dec_ref[:, c].astype(F32)).astype(BF16)
-
-
-def dec_grad_call(feat, err, dec, norm):
-    total, width = err.shape
-    latents = feat.shape[1]
-    tile = 256
-    scale = float(1.0 / (total ** 0.5))
-    return pl.pallas_call(
-        functools.partial(dec_grad_kernel, scale),
-        grid=(latents // tile,),
-        out_shape=jax.ShapeDtypeStruct((latents, width), BF16),
-        in_specs=[
-            pl.BlockSpec((total, tile), lambda i: (0, i)),
-            pl.BlockSpec((total, width), lambda i: (0, 0)),
-            pl.BlockSpec((tile, width), lambda i: (i, 0)),
-            pl.BlockSpec((tile, 1), lambda i: (i, 0)),
-        ],
-        out_specs=pl.BlockSpec((tile, width), lambda i: (i, 0)),
-        compiler_params=pltpu.CompilerParams(vmem_limit_bytes=40 * MIB),
-        cost_estimate=pl.CostEstimate(
-            flops=2 * total * width * latents, bytes_accessed=21 * MIB, transcendentals=0
-        ),
-    )(feat, err, dec, norm)
+            flops=4 * total * width * latents, bytes_accessed=34 * MIB, transcendentals=0
+        ),
+    )(full, rounded, feat, err, dec, norm, bias_grad, dec_bias_grad)
 
 
 def per_device(n, streams, enc_weight, enc_bias, dec_weight, dec_bias):
     decoder = dec_weight[0]
-    row_norm = jnp.sqrt(jnp.sum(jnp.square(decoder.astype(F32)), axis=1) + epsilon_sq)
-    norm_rows = jnp.broadcast_to(row_norm[None, :], (8, row_norm.shape[0]))
-    full, feat, err, rounded, enc_bias_grad, dec_bias_grad = main_call(
-        n, streams[0], enc_weight[0], enc_bias[None, :], decoder, dec_bias, norm_rows
+    full, feat, err, rounded, norm, bias_grad, dec_bias_grad = main_call(
+        n, streams[0], enc_weight[0], enc_bias[None, :], decoder, dec_bias
     )
-    dec_grad = dec_grad_call(feat, err, decoder, row_norm[:, None])
-    enc_grad = enc_grad_call(full, rounded)
-    return (enc_grad[None], enc_bias_grad[0], dec_grad[None], dec_bias_grad)
+    enc_grad, dec_grad, bias_grad, dec_bias_grad = weight_grad_call(
+        full, rounded, feat, err, decoder, norm, bias_grad, dec_bias_grad
+    )
+    return (enc_grad[None], bias_grad[0], dec_grad[None], dec_bias_grad)
 
 
 def solution(mesh):

time: 173 us -> 163 us (0.942)
  local copies, waits for them, and re-layouts: 8.82 us -> 0 us
  other arithmetic: 5.08 us -> 0 us
  Pallas kernels: 159 us -> 162 us
    unnamed x16 -> x0, local copies, waits for them, and re-layouts: 7.98 us -> none
    reduce_sum x1 -> x0, other arithmetic: 5.07 us -> none  [per_device(): jnp.sum(jnp.square(decoder.astype(F32)), axis=1) + epsilon_sq]
    pallas_call x2 -> x1, Pallas kernels: 14.9 us -> 18 us  [weight_grad_call(): pl.pallas_call(functools.partial(weight_grad_kernel, scale), grid=(width...]
where the time goes in v2:
time: 163 us
  Pallas kernels  162 us (99%)
    pallas_call x1, Pallas kernels, main_call(): pl.pallas_call(functools.partial(step_kernel, n), out_shape=(jax.ShapeDty...  144 us
    pallas_call x1, Pallas kernels, weight_grad_call(): pl.pallas_call(functools.partial(weight_grad_kernel, scale), grid=(width...  18 us

profile of v2, /device:TPU:0, one launch (start us, length us, event | category | flops | bytes accessed | tf_op | source)
XLA Modules:
  0.0 162.5 jit_solution(17376117866968810408)
XLA Ops:
  0.6 143.8 %shard_map.84 = (bf16[512,4096]{1,0:T(8,128)(2,1)}, bf16[512,1024]{1,0:T(8,128)(2,1)}, bf16[512,4096]{1,0:T(8,128)(2,1)}, bf16[512,1024]{1,0:T(8,128)(2,1)}, f32...) custom-call(bf16[64,4096]{1,0:T(8,128)(2,1)} %bitcast.10, bf16[4096,1024]{1,0:T(8,128)(2,1)} %bitcast.7, ...), custom_call_target="tpu_custom_call" | custom-call | flops 12884901888 | bytes 33554432 | tf_op jit(solution)/shard_map/pallas_call | solution.py:295
  144.5 18.0 %shard_map.85 = (bf16[4096,1024]{1,0:T(8,128)(2,1)}, bf16[1024,4096]{1,0:T(8,128)(2,1)}, f32[1,1024]{1,0:T(1,128)}, f32[1,512]{1,0:T(1,128)}) custom-call(bf16[512,4096]{1,0:T(8,128)(2,1)} %get-tuple-element.15.full_ref, bf16[512,1024]{1,0:T(8,128)(2,1)} %get-tuple-element.16.round_ref, bf16[512,1024]{1,0:T(8,128)(2,1)} %get-tuple-element.17.feat_ref, ...), custom_call_target="tpu_custom_call" | custom-call | flops 8589934592 | bytes 35651584 | tf_op jit(solution)/shard_map/pallas_call | solution.py:378

commit v3 on v2

--- a/solution.py
+++ b/solution.py
@@ -37,7 +37,7 @@
     full_out, feat_out, err_out, round_out, norm_ref, bias_grad_ref, dec_bias_grad_ref,
     enc, dec, full, part, part_in, pre, feat, partial, sum_right, sum_left, in_right, in_left,
     err, grad, grad_in, rounded, norm_row, norm_in,
-    g_send, g_recv, r_send, r_recv, e_send, e_recv, p_send, p_recv, q_send, q_recv, n_sem, w_sem, o_sem,
+    g_send, g_recv, r_send, r_recv, e_send, e_recv, p_send, p_recv, q_send, q_recv, n_sem, w_sem, o_sem, s_sem,
 ):
     rows, width = x_ref.shape
     latents = enc.shape[1]
@@ -79,7 +79,7 @@
             return n - 1, 1
         return 2 * d - 1, 2
 
-    def gather(buf, s_sem, r_sem, consume):
+    def gather(buf, out_sem, in_sem, consume):
         got = {}
 
         def forward(d, h, way):
@@ -94,7 +94,7 @@
             cols = pl.ds(h * hw, hw)
             got[(d, h, way)] = send(
                 buf.at[slot_rows(src), cols], buf.at[slot_rows(dst), cols],
-                s_sem.at[way, d - 1, h], r_sem.at[way, d - 1, h],
+                out_sem.at[way, d - 1, h], in_sem.at[way, d - 1, h],
                 to_right if way == 0 else to_left,
             )
 
@@ -201,7 +201,7 @@
         decode(d)
         for order in range(2):
             for way in range(2):
-                h = (order + way) % 2
+                h = (order + way + 1) % 2
                 if d == half and h != way:
                     continue
                 base = 0 if d == half or way == 1 else rows
@@ -220,7 +220,7 @@
     decode(0)
     for order in range(2):
         for way in range(2):
-            moving[(1, (order + way) % 2, way)].wait_recv()
+            moving[(1, (order + way + 1) % 2, way)].wait_recv()
 
     @pl.loop(0, rows // 16)
     def _(i):
@@ -232,7 +232,15 @@
 
     norm_swap[0].wait_recv()
     bias_grad_ref[...] = jnp.zeros_like(bias_grad_ref)
+    dec_bias_grad_ref[...] = jnp.zeros_like(dec_bias_grad_ref)
     grad_swaps = {}
+    saves = []
+
+    def save_step(buf, out, d, which):
+        r = slot_rows(*step_span(d))
+        copy = pltpu.make_async_copy(buf.at[r, :], out.at[r, :], s_sem.at[which, d])
+        copy.start()
+        saves.append(copy)
 
     def finish_grad(d):
         slot, count = step_span(d)
@@ -247,6 +255,8 @@
             rounded[r, :] = value.astype(BF16)
             bias_grad_ref[...] += jnp.sum(value, axis=0, keepdims=True)
 
+        save_step(rounded, round_out, d, 1)
+
     def decode_grad(d):
         slot, count = step_span(d)
         r = slot_rows(slot, count)
@@ -259,26 +269,22 @@
             )
 
         grad_swaps[d] = send(grad.at[r, :], grad_in.at[r, :], q_send.at[d], q_recv.at[d], to_other)
+        save_step(err, err_out, d, 0)
+        mine = pl.ds(pl.multiple_of(lat * own, own), own)
+
+        @pl.loop(0, count * rows // 16)
+        def _(i):
+            block = pl.ds(pl.multiple_of(slot * rows + i * 16, 16), 16)
+            dec_bias_grad_ref[...] += jnp.sum(err[block, mine].astype(F32), axis=0, keepdims=True)
+
         if d >= 1:
             finish_grad(d - 1)
 
     gather(err, e_send, e_recv, decode_grad)
-    save_err = pltpu.make_async_copy(err, err_out, o_sem.at[2])
-    save_err.start()
-    mine = pl.ds(pl.multiple_of(lat * own, own), own)
-    dec_bias_grad_ref[...] = jnp.zeros_like(dec_bias_grad_ref)
-
-    @pl.loop(0, total // 64)
-    def _(i):
-        r = pl.ds(pl.multiple_of(i * 64, 64), 64)
-        dec_bias_grad_ref[...] += jnp.sum(err[r, mine].astype(F32), axis=0, keepdims=True)
-
     finish_grad(half)
-    save_round = pltpu.make_async_copy(rounded, round_out, o_sem.at[3])
-    save_round.start()
     for copy in sending:
         copy.wait_send()
-    for save in (save_full, save_feat, save_err, save_round):
+    for save in [save_full, save_feat] + saves:
         save.wait()
 
 
@@ -325,7 +331,7 @@
             pltpu.VMEM((8, latents), F32),
             pltpu.VMEM((8, latents), F32),
             steps, steps, steps, steps, steps, steps, swap, swap, swap, swap,
-            dma((2,)), dma((2,)), dma((4,)),
+            dma((2,)), dma((2,)), dma((2,)), dma((2, half + 1)),
         ],
         compiler_params=pltpu.CompilerParams(
             collective_id=0, has_side_effects=True, vmem_limit_bytes=60 * MIB
@@ -338,46 +344,49 @@
 
 def weight_grad_kernel(
     scale, full_ref, round_ref, feat_ref, err_ref, dec_ref, norm_ref, bias_grad_ref, dec_bias_grad_ref,
-    enc_out, dec_out, bias_grad_out, dec_bias_grad_out, feats, factor,
+    enc_out, dec_out, bias_grad_out, dec_bias_grad_out,
 ):
     total = feat_ref.shape[0]
-    latents, span = dec_ref.shape
+    width = err_ref.shape[1]
 
     @pl.when(pl.program_id(0) == 0)
     def _():
-        feats[...] = feat_ref[...].T
-        sums = jnp.dot(feats[...], jnp.ones((total, 128), BF16), preferred_element_type=F32)
-        factor[...] = penalty_weight * scale * sums / norm_ref[...]
         bias_grad_out[...] = bias_grad_ref[...]
         dec_bias_grad_out[...] = dec_bias_grad_ref[...]
 
     enc_out[...] = lax.dot_general(
         full_ref[...], round_ref[...], (((0,), (0,)), ((), ())), preferred_element_type=F32
     ).astype(BF16)
-    step = min(256, latents)
-    for j in range(latents // step):
-        r = pl.ds(j * step, step)
-        direct = jnp.dot(feats[r, :], err_ref[...], preferred_element_type=F32)
-        shrink = factor[r, :1] * dec_ref[r, :].astype(F32)
-        dec_out[r, :] = (direct + shrink).astype(BF16)
+    feats = feat_ref[...].T
+    sums = jnp.dot(feats, jnp.ones((total, 128), BF16), preferred_element_type=F32)
+    factor = (penalty_weight * scale * sums / norm_ref[...])[:, :1]
+    step = min(1024, width)
+    for j in range(width // step):
+        c = pl.ds(j * step, step)
+        direct = jnp.dot(feats, err_ref[:, c], preferred_element_type=F32)
+        dec_out[:, c] = (direct + factor * dec_ref[:, c].astype(F32)).astype(BF16)
 
 
 def weight_grad_call(full, rounded, feat, err, dec, norm, bias_grad, dec_bias_grad):
     total, width = full.shape
     latents = rounded.shape[1]
     own = dec_bias_grad.shape[1]
-    tile = 512
+    steps = min(4, latents // 128)
+    wide, tall = width // steps, latents // steps
     scale = float(1.0 / (total ** 0.5))
 
     def whole(rows, columns):
         return pl.BlockSpec((rows, columns), lambda i: (0, 0))
 
-    def columns_of(rows):
-        return pl.BlockSpec((rows, tile), lambda i: (0, i))
+    def columns_of(rows, columns):
+        return pl.BlockSpec((rows, columns), lambda i: (0, i))
+
+    def rows_of(rows, columns):
+        return pl.BlockSpec((rows, columns), lambda i: (i, 0))
 
     return pl.pallas_call(
         functools.partial(weight_grad_kernel, scale),
-        grid=(width // tile,),
+        grid=(steps,),
         out_shape=(
             jax.ShapeDtypeStruct((width, latents), BF16),
             jax.ShapeDtypeStruct((latents, width), BF16),
@@ -385,14 +394,13 @@
             jax.ShapeDtypeStruct((1, own), F32),
         ),
         in_specs=[
-            columns_of(total), whole(total, latents), whole(total, latents), columns_of(total),
-            columns_of(latents), whole(latents, 128), whole(1, latents), whole(1, own),
+            columns_of(total, wide), whole(total, latents), columns_of(total, tall), whole(total, width),
+            rows_of(tall, width), rows_of(tall, 128), whole(1, latents), whole(1, own),
         ],
         out_specs=(
-            pl.BlockSpec((tile, latents), lambda i: (i, 0)), columns_of(latents),
+            rows_of(wide, latents), rows_of(tall, width),
             whole(1, latents), whole(1, own),
         ),
-        scratch_shapes=[pltpu.VMEM((latents, total), BF16), pltpu.VMEM((latents, 128), F32)],
         compiler_params=pltpu.CompilerParams(vmem_limit_bytes=60 * MIB),
         cost_estimate=pl.CostEstimate(
             flops=4 * total * width * latents, bytes_accessed=34 * MIB, transcendentals=0

time: 163 us -> 159 us (0.975)
  Pallas kernels: 162 us -> 158 us
    pallas_call x1, Pallas kernels: 144 us -> 142 us  [main_call(): pl.pallas_call(functools.partial(step_kernel, n), out_shape=(jax.ShapeDty...]
    pallas_call x1, Pallas kernels: 18 us -> 16.1 us  [weight_grad_call(): pl.pallas_call(functools.partial(weight_grad_kernel, scale), grid=(steps,...]
where the time goes in v3:
time: 159 us; the launch traced here: 158 us
  Pallas kernels  158 us (99%)
    pallas_call x1, Pallas kernels, main_call(): pl.pallas_call(functools.partial(step_kernel, n), out_shape=(jax.ShapeDty...  142 us
    pallas_call x1, Pallas kernels, weight_grad_call(): pl.pallas_call(functools.partial(weight_grad_kernel, scale), grid=(steps,...  16.1 us

profile of v3, /device:TPU:0, one launch (start us, length us, event | category | flops | bytes accessed | tf_op | source)
XLA Modules:
  0.0 158.3 jit_solution(8816753934102464555)
XLA Ops:
  0.6 141.6 %shard_map.84 = (bf16[512,4096]{1,0:T(8,128)(2,1)}, bf16[512,1024]{1,0:T(8,128)(2,1)}, bf16[512,4096]{1,0:T(8,128)(2,1)}, bf16[512,1024]{1,0:T(8,128)(2,1)}, f32...) custom-call(bf16[64,4096]{1,0:T(8,128)(2,1)} %bitcast.10, bf16[4096,1024]{1,0:T(8,128)(2,1)} %bitcast.7, ...), custom_call_target="tpu_custom_call" | custom-call | flops 12884901888 | bytes 33554432 | tf_op jit(solution)/shard_map/pallas_call | solution.py:301
  142.2 16.1 %shard_map.85 = (bf16[4096,1024]{1,0:T(8,128)(2,1)}, bf16[1024,4096]{1,0:T(8,128)(2,1)}, f32[1,1024]{1,0:T(1,128)}, f32[1,512]{1,0:T(1,128)}) custom-call(bf16[512,4096]{1,0:T(8,128)(2,1)} %get-tuple-element.15.full_ref, bf16[512,1024]{1,0:T(8,128)(2,1)} %get-tuple-element.16.round_ref, bf16[512,1024]{1,0:T(8,128)(2,1)} %get-tuple-element.17.feat_ref, ...), custom_call_target="tpu_custom_call" | custom-call | flops 8589934592 | bytes 35651584 | tf_op jit(solution)/shard_map/pallas_call | solution.py:387

commit v4 on v3

--- a/solution.py
+++ b/solution.py
@@ -152,7 +152,7 @@
         slot, count = step_span(d)
         r = slot_rows(slot, count)
 
-        @pl.loop(0, latents // tile)
+        @pl.loop(0, latents // tile, unroll=True)
         def _(j):
             c = pl.ds(pl.multiple_of(j * tile, tile), tile)
             part[r, c] = jnp.dot(full[r, :], enc[:, c], preferred_element_type=F32)
@@ -178,7 +178,7 @@
         r = slot_rows(slot, count)
         to = pl.ds(0, count * rows)
 
-        @pl.loop(0, width // wide)
+        @pl.loop(0, width // wide, unroll=2)
         def _(j):
             c = pl.ds(pl.multiple_of(j * wide, wide), wide)
             partial[to, c] = jnp.dot(feat[r, :], dec[:, c], preferred_element_type=F32)
@@ -261,7 +261,7 @@
         slot, count = step_span(d)
         r = slot_rows(slot, count)
 
-        @pl.loop(0, latents // tile)
+        @pl.loop(0, latents // tile, unroll=True)
         def _(j):
             c = pl.ds(pl.multiple_of(j * tile, tile), tile)
             grad[r, c] = lax.dot_general(

time: 159 us -> 157 us (0.987)
  Pallas kernels: 158 us -> 156 us
    pallas_call x1, Pallas kernels: 142 us -> 140 us  [main_call(): pl.pallas_call(functools.partial(step_kernel, n), out_shape=(jax.ShapeDty...]
where the time goes in v4:
time: 157 us
  Pallas kernels  156 us (99%)
    pallas_call x1, Pallas kernels, main_call(): pl.pallas_call(functools.partial(step_kernel, n), out_shape=(jax.ShapeDty...  140 us
    pallas_call x1, Pallas kernels, weight_grad_call(): pl.pallas_call(functools.partial(weight_grad_kernel, scale), grid=(steps,...  16.1 us

profile of v4, /device:TPU:0, one launch (start us, length us, event | category | flops | bytes accessed | tf_op | source)
XLA Modules:
  0.0 156.7 jit_solution(1878426074170657098)
XLA Ops:
  0.6 140.0 %shard_map.84 = (bf16[512,4096]{1,0:T(8,128)(2,1)}, bf16[512,1024]{1,0:T(8,128)(2,1)}, bf16[512,4096]{1,0:T(8,128)(2,1)}, bf16[512,1024]{1,0:T(8,128)(2,1)}, f32...) custom-call(bf16[64,4096]{1,0:T(8,128)(2,1)} %bitcast.10, bf16[4096,1024]{1,0:T(8,128)(2,1)} %bitcast.7, ...), custom_call_target="tpu_custom_call" | custom-call | flops 12884901888 | bytes 33554432 | tf_op jit(solution)/shard_map/pallas_call | solution.py:301
  140.6 16.1 %shard_map.85 = (bf16[4096,1024]{1,0:T(8,128)(2,1)}, bf16[1024,4096]{1,0:T(8,128)(2,1)}, f32[1,1024]{1,0:T(1,128)}, f32[1,512]{1,0:T(1,128)}) custom-call(bf16[512,4096]{1,0:T(8,128)(2,1)} %get-tuple-element.15.full_ref, bf16[512,1024]{1,0:T(8,128)(2,1)} %get-tuple-element.16.round_ref, bf16[512,1024]{1,0:T(8,128)(2,1)} %get-tuple-element.17.feat_ref, ...), custom_call_target="tpu_custom_call" | custom-call | flops 8589934592 | bytes 35651584 | tf_op jit(solution)/shard_map/pallas_call | solution.py:387
